TPU v7x, 32 devices: a whole 2x2x4 slice. The times are simulated.
32 devices in a mesh: grp: 2 (over x), gx: 16 (over z, y, core).
Axes of the slice: x: 2, y: 2, z: 4, core: 2. Of those that a mesh axis runs over, the one named last changes fastest.
Arguments:
- hidden_in: bfloat16 [8, 16384], P('grp', 'gx'), parts along dimension 0, may hold values from -128 to 128
- norm_gain: bfloat16 [16384], P('gx'), may hold values from 0.099609375 to 1.8984375
- qkv_weight: bfloat16 [16384, 4, 2304], P('gx'), may hold values from -0.046875 to 0.046875
- out_weight: bfloat16 [8192, 16384], P(None, 'gx'), may hold values from -0.0625 to 0.0625
- key_cache: bfloat16 [32, 8192, 128], P(('grp', 'gx')), parts along dimension 0, may hold values from -400 to 400
- value_cache: bfloat16 [32, 8192, 128], P(('grp', 'gx')), parts along dimension 0, may hold values from -6 to 6
- lengths: int32 [8], P('grp'), parts along dimension 0, may hold values from 1024 to 8192, as said below
- positions: int32 [8], P('grp'), parts along dimension 0, may hold values from 0 to 8191
Outputs:
- attention_out: bfloat16 [8, 16384], P('grp', 'gx'), parts along dimension 0
- new_entry: bfloat16 [32, 256], P(('grp', 'gx')), parts along dimension 0
There are 2 independent parts, one for each index of `grp`. A program takes and returns all parts, laid end to end along the dimension named above; an argument that names none is the same for every part. Nothing has to cross between parts.
Inputs may be any that keep to these rules, and one draw needn't show every extreme that they name: `lengths`: some row reaches 8192.
All inputs are finite; a program needn't handle non-finite values.
Results may differ from a plain program's by a relative error of at most 0.012.
Values may be sent and summed in bfloat16 or wider, within the bound.
A program may use at most 128 MiB of HBM per device.

v0:
```python
import jax
import jax.numpy as jnp
from jax import lax
from jax.sharding import PartitionSpec as P

rope_base = 500000.0
norm_eps = 1e-05


def rotate(vectors, places):
    half_width = vectors.shape[-1] // 2
    frequency = rope_base ** (
        -(jnp.arange(half_width, dtype=jnp.float32) * 2.0 / vectors.shape[-1])
    )
    angles = places.astype(jnp.float32)[:, None] * frequency[None, :]
    cosine = jnp.cos(angles)[:, None, :]
    sine_part = jnp.sin(angles)[:, None, :]
    front_half = vectors[..., :half_width]
    second = vectors[..., half_width:]
    return jnp.concatenate(
        [front_half * cosine - second * sine_part, second * cosine + front_half * sine_part],
        axis=-1,
    )


def attend(packed):
    queries, cached_keys, cached_values, own_key, own_value, length = packed
    score_scale = queries.shape[-1] ** (-0.5)
    scores = jnp.dot(queries, cached_keys.T, preferred_element_type=jnp.float32) * score_scale
    in_range = jnp.arange(cached_keys.shape[0], dtype=jnp.int32) < length
    scores = jnp.where(in_range[None, :], scores, -jnp.inf)
    own_score = jnp.dot(queries, own_key, preferred_element_type=jnp.float32) * score_scale
    highest = jnp.maximum(jnp.max(scores, axis=1), own_score)
    exponent = jnp.exp(scores - highest[:, None])
    own_exponent = jnp.exp(own_score - highest)
    denominator = jnp.sum(exponent, axis=1) + own_exponent
    weights = (exponent / denominator[:, None]).astype(jnp.bfloat16)
    own_weight = (own_exponent / denominator).astype(jnp.bfloat16)
    combined = jnp.dot(weights, cached_values, preferred_element_type=jnp.float32)
    combined = (
        combined + own_weight.astype(jnp.float32)[:, None] * own_value.astype(jnp.float32)[None, :]
    )
    return combined.reshape(-1).astype(jnp.bfloat16)


def local(hidden_in, norm_gain, qkv_weight, out_weight, key_cache, value_cache, lengths, positions):
    devices = lax.axis_size("gx")
    device_index = lax.axis_index("gx")
    row_count = hidden_in.shape[0]
    features = hidden_in.astype(jnp.float32)
    squares = lax.psum(jnp.sum(features * features, axis=1), "gx")
    inverse = lax.rsqrt(squares / (features.shape[1] * devices) + norm_eps)
    normed = (features * inverse[:, None] * norm_gain.astype(jnp.float32)[None, :]).astype(
        jnp.bfloat16
    )
    kv_heads = qkv_weight.shape[1]
    columns = qkv_weight.shape[2]
    partial_term = jnp.einsum("rd,dhc->hrc", normed, qkv_weight, preferred_element_type=jnp.float32)
    partial_term = partial_term.reshape(kv_heads * row_count, columns)
    slot_count = key_cache.shape[0]
    summed = lax.psum(partial_term, "gx")
    projected = lax.dynamic_slice_in_dim(summed, device_index * slot_count, slot_count, 0)
    head_dim = key_cache.shape[2]
    group_width = columns - 2 * head_dim
    slot_ids = device_index * slot_count + jnp.arange(slot_count, dtype=jnp.int32)
    row_ids = slot_ids % row_count
    places = positions[row_ids]
    limits = lengths[row_ids]
    queries = rotate(
        projected[:, :group_width].reshape(slot_count, group_width // head_dim, head_dim), places
    ).astype(jnp.bfloat16)
    new_keys = rotate(projected[:, group_width : group_width + head_dim][:, None, :], places)[
        :, 0, :
    ].astype(jnp.bfloat16)
    new_values = projected[:, group_width + head_dim :].astype(jnp.bfloat16)
    new_entry = jnp.concatenate([new_keys, new_values], axis=1)
    heads_block = lax.map(attend, (queries, key_cache, value_cache, new_keys, new_values, limits))
    everything = lax.all_gather(heads_block, "gx", axis=0, tiled=True)
    grouped = everything.reshape(kv_heads, row_count, group_width)
    weight_groups = out_weight.reshape(kv_heads, group_width, out_weight.shape[1])
    summed_out = jnp.einsum(
        "hrk,hkc->rc", grouped, weight_groups, preferred_element_type=jnp.float32
    )
    attention_out = summed_out.astype(jnp.bfloat16)
    return (attention_out, new_entry)


def solution(mesh):
    in_specs = (
        P("grp", "gx"),
        P("gx"),
        P("gx", None, None),
        P(None, "gx"),
        P(("grp", "gx"), None, None),
        P(("grp", "gx"), None, None),
        P("grp"),
        P("grp"),
    )
    out_specs = (P("grp", "gx"), P(("grp", "gx"), None))
    return jax.shard_map(local, mesh=mesh, in_specs=in_specs, out_specs=out_specs, check_vma=False)
```

profile of v0, /device:TPU:0, one launch (start us, length us, event | category | flops | bytes accessed | tf_op | source)
XLA Modules:
  0.0 182.8 jit_solution(2995393362002717977)
XLA Ops:
  7.2 1.0 fusion.20
  8.2 34.9 %psum.14 = f32[4]{0:T(128)S(1)} all-reduce(f32[4]{0:T(128)S(1)} %fusion.20), channel_id=1, replica_groups=mesh['grp'=2,'gx'=16] {'gx'}, use_global_device_ids=true, to_apply=%region_1.0 | all-reduce | flops 4 | bytes 32 | tf_op jit(solution)/shard_map/psum | solution.py:51
  43.1 0.7 convert_element_type.69
  43.8 9.0 %fusion.3 = f32[4,4,2304]{2,1,0:T(4,128)S(1)} fusion(bf16[1024,4,2304]{2,1,0:T(4,128)(2,1)} %param.10, bf16[4,1024]{1,0:T(4,128)(2,1)} %param.8, f32[1024]{0:T(1024)S(1)} %convert_element_type.69, f32[4]{0:T(128)S(1)} %add_rsqrt_fusion), kind=kOutput, calls=%fused_computation.4 | convolution fusion | flops 75513856 | bytes 19034128 | tf_op jit(solution)/shard_map/rd,dhc->hrc/dot_general | solution.py:58
  52.8 0.7 reshape.105
  53.5 0.7 dynamic-slice.5
  54.9 0.7 dynamic-slice.4
  55.6 0.7 iota_compare_fusion
  56.3 0.1 fusion.32
  56.3 82.4 %all-reduce.2.cloned.1.call-done = f32[16,2304]{1,0:T(8,128)} async-done(((f32[16,2304]{1,0:T(8,128)}), f32[16,2304]{1,0:T(8,128)}) %all-reduce.2.cloned.1.call-update) | async-done | bytes 147472 | tf_op jit(solution)/shard_map/psum | solution.py:61
  138.7 0.7 dynamic-slice_bitcast_fusion
  139.5 0.1 multiply_subtract_fusion
  139.5 0.1 fusion.37
  139.6 0.9 constant_dynamic-slice_fusion
  140.5 0.1 fusion.27
  140.6 0.8 fusion.38
  141.4 0.2 fusion.39
  141.6 0.3 fusion.17
  141.9 0.8 bitcast_convert_fusion
  142.6 2.0 %fusion.13 = bf16[16,128]{1,0:T(8,128)(2,1)S(1)} fusion(bf16[1,8192,128]{2,1,0:T(8,128)(2,1)} %param.13, f32[16,8192]{1,0:T(8,128)S(1)} %get-tuple-element.57, f32[16]{0:T(128)S(1)} %get-tuple-element.53, f32[16]{0:T(128)S(1)} %get-tuple-element.58, f32[128]{0:T(128)S(1)} %get-tuple-element.48, f32[16]{0:T(128)S(1)} %get-tuple-element.52), kind=kOutput, calls=%fused_computation.11 | convolution fusion | flops 33953792 | bytes 2626240 | tf_op jit(solution)/shard_map/while/body/eval_jaxpr/dot_general | solution.py:39
  144.7 21.7 %all-gather = bf16[16,1,2048]{2,1,0:T(2,128)(2,1)S(1)} all-gather(bf16[1,1,2048]{2,1,0:T(2,128)(2,1)S(1)} %reshape.151), channel_id=1, replica_groups=mesh['grp'=2,'gx'=16] {'gx'}, dimensions={0}, use_global_device_ids=true | all-gather | bytes 69632 | tf_op jit(solution)/shard_map/all_gather | solution.py:78
  166.4 0.4 reduce
  166.8 0.6 pad_maximum_fusion.1
  167.3 8.6 %fusion.9 = bf16[4,1024]{1,0:T(4,128)(2,1)} fusion(bf16[4,4,2048]{2,1,0:T(4,128)(2,1)S(1)} %reshape.107, bf16[4,2048,1024]{2,1,0:T(8,128)(2,1)} %bitcast.51), kind=kOutput, calls=%fused_computation.9 | convolution fusion | flops 67112960 | bytes 16850944 | tf_op jit(solution)/shard_map/hrk,hkc->rc/dot_general | solution.py:81
  (12 shorter events, 0.1 us)
Async XLA Ops:
  7.2 133.4 %copy-start = (bf16[1,8192,128]{2,1,0:T(8,128)(2,1)S(1)}, bf16[1,8192,128]{2,1,0:T(8,128)(2,1)}, u32[]{:S(2)}) copy-start(bf16[1,8192,128]{2,1,0:T(8,128)(2,1)} %param.12) | copy-start | bytes 6291460
  7.2 46.4 %copy-start.1 = (s32[4]{0:T(128)S(1)}, s32[4]{0:T(128)}, u32[]{:S(2)}) copy-start(s32[4]{0:T(128)} %param.15) | copy-start | bytes 52
  7.2 47.7 %copy-start.2 = (s32[4]{0:T(128)S(1)}, s32[4]{0:T(128)}, u32[]{:S(2)}) copy-start(s32[4]{0:T(128)} %param.14) | copy-start | bytes 52
  7.2 131.5 %all-reduce.2.cloned.1.call-start = ((), (), s32[]{:S(2)}) async-start(), calls=%async_computation | async-start | bytes 294912 | tf_op jit(solution)/shard_map/psum | solution.py:61
Sparse Core Ops, SparseCore 0:
  53.6 85.0 all-reduce.1
where the time goes:
time: 183 us
  waiting for transfers between devices  82.4 us (45%)
  blocking collectives  56.6 us (31%)
  matrix products  20.7 us (11%)
  between operations  14.8 us (8%)
  other arithmetic  4.62 us (3%)
  local copies, waits for them, and re-layouts  3.7 us (2%)
    psum x1, waiting for transfers between devices, local(): summed = lax.psum(partial_term, 'gx')  82.4 us
    psum x1, blocking collectives, local(): squares = lax.psum(jnp.sum(features * features, axis=1), 'gx')  34.9 us
    all_gather x1, blocking collectives, local(): everything = lax.all_gather(heads_block, 'gx', axis=0, tiled=True)  21.7 us
    dot_general x1, matrix products, local(): jnp.einsum('rd,dhc->hrc', normed, qkv_weight, preferred_element_type=jnp....  8.96 us
    dot_general x1, matrix products, local(): jnp.einsum('hrk,hkc->rc', grouped, weight_groups, preferred_element_type=...  8.65 us
  transfers between devices with their start and end apart: 1, of which 1 were waited for; matrix products, arithmetic and copies ran while one was open for 1% of the time, Pallas kernels for 0%

commit v1 on v0

v1 whole, which is shorter than its diff:
```python
import functools

import jax
import jax.numpy as jnp
import numpy as np
from jax import lax
from jax.experimental import pallas as pl
from jax.experimental.pallas import tpu as pltpu
from jax.sharding import PartitionSpec as P

rope_base = 500000.0
norm_eps = 1e-05
MESH = pl.DeviceIdType.MESH
KEY_CHUNKS = 4
WEIGHT_CHUNKS = 16
MSG_ROWS = 32


def attention_kernel(
    n, kv_heads, row_count, features_total,
    lengths_ref, positions_ref, freq_ref, hidden_ref, gain_ref, p_hbm, k_hbm, v_hbm, w_hbm,
    out_ref, entry_ref,
    p_vmem, lhs_ref, part_ref, k_vmem, v_vmem, w_vmem, wide, send_buf, recv_buf, heads_own, heads_all, score_buf, lhs_buf,
    p_sem, k_sem, v_sem, w_sem, psend_sem, precv_sem, hsend_sem, hrecv_sem,
):
    me = lax.axis_index("gx")
    head_dim = k_hbm.shape[2]
    ctx = k_hbm.shape[1]
    half = head_dim // 2
    slots = kv_heads * row_count
    groups = part_ref.shape[1] // head_dim - 2
    depth = w_hbm.shape[0]

    k_len = ctx // KEY_CHUNKS
    w_len = depth // WEIGHT_CHUNKS

    local_d = hidden_ref.shape[1]
    d_len = min(head_dim, local_d)
    p_chunks = local_d // d_len

    def proj_copy(c):
        rows = pl.ds(c * d_len, d_len)
        return pltpu.make_async_copy(p_hbm.at[rows], p_vmem.at[rows], p_sem.at[c])

    def key_copy(c):
        rows = pl.ds(c * k_len, k_len)
        return pltpu.make_async_copy(k_hbm.at[0, rows, :], k_vmem.at[rows, :], k_sem.at[c])

    def value_copy(c):
        rows = pl.ds(c * k_len, k_len)
        return pltpu.make_async_copy(v_hbm.at[0, rows, :], v_vmem.at[rows, :], v_sem.at[c])

    def weight_copy(c):
        rows = pl.ds(c * w_len, w_len)
        return pltpu.make_async_copy(w_hbm.at[rows, :], w_vmem.at[rows, :], w_sem.at[c])

    for c in range(p_chunks):
        proj_copy(c).start()

    barrier = pltpu.get_barrier_semaphore()

    @pl.loop(1, n)
    def _(i):
        pl.semaphore_signal(
            barrier, inc=1, device_id={"gx": lax.rem(me + i, n)}, device_id_type=MESH
        )

    for c in range(KEY_CHUNKS):
        key_copy(c).start()
    for c in range(KEY_CHUNKS):
        value_copy(c).start()
    for c in range(WEIGHT_CHUNKS):
        weight_copy(c).start()

    x = hidden_ref[...].astype(jnp.float32)
    scaled = x * gain_ref[...].astype(jnp.float32)
    high = scaled.astype(jnp.bfloat16)
    low = (scaled - high.astype(jnp.float32)).astype(jnp.bfloat16)
    span = d_len * kv_heads
    spread = (
        lax.broadcasted_iota(jnp.int32, (d_len, span), 1) // kv_heads
        == lax.broadcasted_iota(jnp.int32, (d_len, span), 0)
    ).astype(jnp.float32).astype(jnp.bfloat16)
    own_head = (
        lax.broadcasted_iota(jnp.int32, (slots, span), 1) % kv_heads
        == lax.broadcasted_iota(jnp.int32, (slots, span), 0) // row_count
    )
    for c in range(p_chunks):
        for half_index, piece in enumerate((high, low)):
            piece = piece[:, c * d_len:(c + 1) * d_len]
            wide_piece = jnp.dot(piece, spread, preferred_element_type=jnp.float32)
            wide_piece = jnp.concatenate([wide_piece] * kv_heads, axis=0)
            lhs_ref[c, half_index * slots:(half_index + 1) * slots, :] = jnp.where(
                own_head, wide_piece, 0.0
            ).astype(jnp.bfloat16)
    columns = p_hbm.shape[2]
    for c in range(p_chunks):
        proj_copy(c).wait()
        lhs = lhs_ref[c]
        for t in range(0, columns, 256):
            tile = p_vmem[c * d_len:(c + 1) * d_len, :, t:t + 256].reshape(span, 256)
            both = jnp.dot(lhs, tile, preferred_element_type=jnp.float32)
            both = both[:slots] + both[slots:]
            if c == 0:
                part_ref[:, t:t + 256] = both
            else:
                part_ref[:, t:t + 256] += both

    squares = jnp.sum(x * x, axis=1, keepdims=True)
    squares = jnp.concatenate([squares] * kv_heads, axis=0)
    squares = jnp.broadcast_to(squares, (slots, head_dim))
    sq_high = squares.astype(jnp.bfloat16).astype(jnp.float32)
    for g in range(groups + 2):
        wide[:, g, :] = part_ref[:, g * head_dim:(g + 1) * head_dim]
    wide[:, groups + 2, :] = sq_high
    wide[:, groups + 3, :] = squares - sq_high
    for g in range(groups + 4, MSG_ROWS):
        wide[:, g, :] = jnp.zeros((slots, head_dim), jnp.float32)
    send_buf[...] = wide[...].astype(jnp.bfloat16)

    pl.semaphore_wait(barrier, n - 1)

    def part_copy(i):
        peer = lax.rem(me + i, n)
        return pltpu.make_async_remote_copy(
            src_ref=send_buf.at[peer],
            dst_ref=recv_buf.at[i],
            send_sem=psend_sem.at[i],
            recv_sem=precv_sem.at[i],
            device_id={"gx": peer},
            device_id_type=MESH,
        )

    @pl.loop(1, n)
    def _(i):
        part_copy(i).start()

    recv_buf[0] = send_buf[me]

    row = lax.rem(me, row_count)
    place = positions_ref[row].astype(jnp.float32)
    limit = lengths_ref[row]
    angles = freq_ref[...] * place
    cosine = jnp.cos(angles)
    sine = jnp.sin(angles)
    lane = lax.broadcasted_iota(jnp.int32, (1, head_dim), 1)
    sine = jnp.where(lane < half, -sine, sine)

    @pl.loop(1, n)
    def _(i):
        part_copy(i).wait_recv()

    total = jnp.sum(recv_buf[...].astype(jnp.float32), axis=0)
    square_sum = total[groups + 2:groups + 3, :] + total[groups + 3:groups + 4, :]
    projected = total * lax.rsqrt(square_sum / features_total + norm_eps)
    turned = (projected * cosine + pltpu.roll(projected, half, 1) * sine).astype(jnp.bfloat16)
    queries = turned[:groups, :]
    own_key = turned[groups:groups + 1, :]
    own_value = projected[groups + 1:groups + 2, :].astype(jnp.bfloat16)
    entry_ref[...] = jnp.concatenate([own_key, own_value], axis=1)

    scale = head_dim ** (-0.5)
    own_score = (
        jnp.sum(
            queries.astype(jnp.float32) * own_key.astype(jnp.float32), axis=1, keepdims=True
        )
        * scale
    )
    highest = own_score
    for c in range(KEY_CHUNKS):
        key_copy(c).wait()
        s = lax.dot_general(
            queries, k_vmem[c * k_len:(c + 1) * k_len, :], (((1,), (1,)), ((), ())),
            preferred_element_type=jnp.float32,
        ) * scale
        token = c * k_len + lax.broadcasted_iota(jnp.int32, (1, k_len), 1)
        s = jnp.where(token < limit, s, -1e30)
        score_buf[:, c * k_len:(c + 1) * k_len] = s
        highest = jnp.maximum(highest, jnp.max(s, axis=1, keepdims=True))
    own_weight = jnp.exp(own_score - highest)
    denominator = own_weight
    combined = own_weight * own_value.astype(jnp.float32)
    for c in range(KEY_CHUNKS):
        value_copy(c).wait()
        p = jnp.exp(score_buf[:, c * k_len:(c + 1) * k_len] - highest)
        denominator = denominator + jnp.sum(p, axis=1, keepdims=True)
        combined = combined + jnp.dot(
            p.astype(jnp.bfloat16), v_vmem[c * k_len:(c + 1) * k_len, :],
            preferred_element_type=jnp.float32,
        )
    heads_own[...] = (combined / denominator).astype(jnp.bfloat16)

    def heads_copy(i):
        peer = lax.rem(me + i, n)
        return pltpu.make_async_remote_copy(
            src_ref=heads_own,
            dst_ref=heads_all.at[me],
            send_sem=hsend_sem.at[i],
            recv_sem=hrecv_sem.at[me],
            device_id={"gx": peer},
            device_id_type=MESH,
        )

    @pl.loop(1, n)
    def _(i):
        heads_copy(i).start()

    heads_all[me] = heads_own[...]

    for c in range(WEIGHT_CHUNKS):
        weight_copy(c).wait()

    @pl.loop(1, n)
    def _(i):
        source = lax.rem(me + i, n)
        pltpu.make_async_remote_copy(
            src_ref=heads_own,
            dst_ref=heads_all.at[source],
            send_sem=hsend_sem.at[i],
            recv_sem=hrecv_sem.at[source],
            device_id={"gx": source},
            device_id_type=MESH,
        ).wait_recv()

    acc = jnp.zeros(out_ref.shape, jnp.float32)
    width = groups * head_dim
    for h in range(kv_heads):
        block = heads_all[h * row_count:(h + 1) * row_count].astype(jnp.float32)
        for g in range(groups):
            lhs_buf[:, g * head_dim:(g + 1) * head_dim] = block[:, g, :]
        acc = acc + jnp.dot(
            lhs_buf[...].astype(jnp.bfloat16), w_vmem[h * width:(h + 1) * width, :],
            preferred_element_type=jnp.float32,
        )
    out_ref[...] = acc.astype(jnp.bfloat16)

    @pl.loop(1, n)
    def _(i):
        part_copy(i).wait_send()
        heads_copy(i).wait_send()


def local(n, hidden_in, norm_gain, qkv_weight, out_weight, key_cache, value_cache, lengths, positions):
    row_count, local_features = hidden_in.shape
    kv_heads, columns = qkv_weight.shape[1:]
    slot_count, ctx, head_dim = key_cache.shape
    slots = kv_heads * row_count
    assert slot_count == 1 and slots == n
    groups = columns // head_dim - 2
    width = groups * head_dim
    d_len = min(head_dim, local_features)
    p_chunks = local_features // d_len
    index = np.arange(head_dim) % (head_dim // 2)
    freq = jnp.asarray((rope_base ** (-(index * 2.0 / head_dim)))[None, :], jnp.float32)
    vmem = pl.BlockSpec(memory_space=pltpu.VMEM)
    smem = pl.BlockSpec(memory_space=pltpu.SMEM)
    hbm = pl.BlockSpec(memory_space=pl.ANY)
    depth, out_columns = out_weight.shape
    dma = pltpu.SemaphoreType.DMA
    return pl.pallas_call(
        functools.partial(attention_kernel, n, kv_heads, row_count, local_features * n),
        out_shape=(
            jax.ShapeDtypeStruct((row_count, out_columns), jnp.bfloat16),
            jax.ShapeDtypeStruct((1, 2 * head_dim), jnp.bfloat16),
        ),
        in_specs=[smem, smem, vmem, vmem, vmem, hbm, hbm, hbm, hbm],
        out_specs=(vmem, vmem),
        scratch_shapes=[
            pltpu.VMEM(qkv_weight.shape, jnp.bfloat16),
            pltpu.VMEM((p_chunks, 2 * slots, d_len * kv_heads), jnp.bfloat16),
            pltpu.VMEM((slots, columns), jnp.float32),
            pltpu.VMEM((ctx, head_dim), jnp.bfloat16),
            pltpu.VMEM((ctx, head_dim), jnp.bfloat16),
            pltpu.VMEM((depth, out_columns), jnp.bfloat16),
            pltpu.VMEM((slots, MSG_ROWS, head_dim), jnp.float32),
            pltpu.VMEM((slots, MSG_ROWS, head_dim), jnp.bfloat16),
            pltpu.VMEM((n, MSG_ROWS, head_dim), jnp.bfloat16),
            pltpu.VMEM((groups, head_dim), jnp.bfloat16),
            pltpu.VMEM((n, groups, head_dim), jnp.bfloat16),
            pltpu.VMEM((groups, ctx), jnp.float32),
            pltpu.VMEM((row_count, width), jnp.float32),
            dma((p_chunks,)),
            dma((KEY_CHUNKS,)),
            dma((KEY_CHUNKS,)),
            dma((WEIGHT_CHUNKS,)),
            dma((n,)),
            dma((n,)),
            dma((n,)),
            dma((n,)),
        ],
        compiler_params=pltpu.CompilerParams(
            collective_id=0, has_side_effects=True, vmem_limit_bytes=60 * 1024 * 1024
        ),
    )(lengths, positions, freq, hidden_in, norm_gain[None, :], qkv_weight, key_cache, value_cache, out_weight)


def solution(mesh):
    in_specs = (
        P("grp", "gx"),
        P("gx"),
        P("gx", None, None),
        P(None, "gx"),
        P(("grp", "gx"), None, None),
        P(("grp", "gx"), None, None),
        P("grp"),
        P("grp"),
    )
    out_specs = (P("grp", "gx"), P(("grp", "gx"), None))
    return jax.shard_map(
        functools.partial(local, mesh.shape["gx"]),
        mesh=mesh, in_specs=in_specs, out_specs=out_specs, check_vma=False,
    )
```

time: 183 us -> 30.3 us (0.17)
  waiting for transfers between devices: 82.4 us -> 0 us
  blocking collectives: 56.6 us -> 0 us
  Pallas kernels: 0 us -> 25.6 us
  matrix products: 20.7 us -> 0 us
  between operations: 14.8 us -> 0.64 us
  other arithmetic: 4.62 us -> 0 us
    psum x1 -> x0, waiting for transfers between devices: 82.4 us -> none  [local(): summed = lax.psum(partial_term, 'gx')]
    psum x1 -> x0, blocking collectives: 34.9 us -> none  [local(): squares = lax.psum(jnp.sum(features * features, axis=1), 'gx')]
    pallas_call x0 -> x1, Pallas kernels: none -> 25.6 us  [local(): pl.pallas_call(functools.partial(attention_kernel, n, kv_heads, row_count...]
    all_gather x1 -> x0, blocking collectives: 21.7 us -> none  [local(): everything = lax.all_gather(heads_block, 'gx', axis=0, tiled=True)]
    dot_general x5 -> x0, matrix products: 20.7 us -> none  [the longest x1 8.96 us: local(): jnp.einsum('rd,dhc->hrc', normed, qkv_weight, preferred_element_type=jnp....]
    unnamed x7 -> x2, local copies, waits for them, and re-layouts: 0.03 us -> 2.52 us
  transfers between devices with their start and end apart: 1 -> 0, of which waited for: 1 -> 0; matrix products, arithmetic and copies ran while one was open for 1% -> 0% of each run, Pallas kernels for 0% -> 0%
where the time goes in v1:
time: 30.3 us; the launch traced here: 30 us
  Pallas kernels  25.6 us (84%)
  local copies, waits for them, and re-layouts  3.79 us (13%)
  between operations  0.64 us (2%)
    pallas_call x1, Pallas kernels, local(): pl.pallas_call(functools.partial(attention_kernel, n, kv_heads, row_count...  25.6 us
    unnamed x2, local copies, waits for them, and re-layouts  2.52 us
    broadcast_in_dim x1, local copies, waits for them, and re-layouts, local(): norm_gain[None, :]  1.28 us

profile of v1, /device:TPU:0, one launch (start us, length us, event | category | flops | bytes accessed | tf_op | source)
XLA Modules:
  0.0 30.0 jit_solution(15157941610739302989)
XLA Ops:
  0.6 1.3 %broadcast_in_dim.3.gain_ref = bf16[1,1024]{1,0:T(2,128)(2,1)} reshape(bf16[1024]{0:T(1024)(128)(2,1)} %param.10) | data formatting | bytes 4096 | tf_op jit(solution)/shard_map/broadcast_in_dim | solution.py:294
  1.9 25.6 %shard_map.104 = (bf16[4,1024]{1,0:T(4,128)(2,1)}, bf16[1,256]{1,0:T(2,128)(2,1)}) custom-call(s32[4]{0:T(128)} %lengths_ref.1, s32[4]{0:T(128)} %positions_ref.1, f32[1,128]{1,0:T(1,128)} %constant.2.clone.freq_ref, bf16[4,1024]{1,0:T(4,128)(2,1)} %hidden_ref.1, bf16[1,1024]{1,0:T(2,128)(2,1)} %broadcast_in_dim.3.gain_ref, bf16[1024,4,2304]{2,1,0:T(4,128)(2,1)} %p_hbm.1, ...), custom_call_target="tpu_custom_call" | custom-call | tf_op jit(solution)/shard_map/pallas_call | solution.py:260
  27.5 1.3 %copy.13 = bf16[4,1024]{1,0:T(4,128)(2,1)} copy(bf16[4,1024]{1,0:T(4,128)(2,1)} %get-tuple-element.4) | data formatting | bytes 16384
  28.8 1.2 %copy.14 = bf16[1,256]{1,0:T(2,128)(2,1)} copy(bf16[1,256]{1,0:T(2,128)(2,1)} %get-tuple-element.5) | data formatting | bytes 1024
